TPU v7x, 32 devices: a whole 2x2x4 slice. The times are simulated.
32 devices in a mesh: orb: 8 (over y, x, core), probe: 4 (over z).
Axes of the slice: x: 2, y: 2, z: 4, core: 2. Of those that a mesh axis runs over, the one named last changes fastest.
Arguments:
- tiles: bfloat16 [32, 9, 256, 256], P('orb', None, 'probe'), may hold values from -0.0625 to 0.0625
- pattern: int32 [32, 9], P('orb'), may hold values from 0 to 1, as said below
- signs: int32 [8192, 512], P('orb', 'probe'), may hold values from 0 to 1
- previous: bfloat16 [8192, 512], P('orb', 'probe'), may hold values from -6 to 6
- current: bfloat16 [8192, 512], P('orb', 'probe'), may hold values from -6 to 6
Outputs:
- older: bfloat16 [8192, 512], P('orb', 'probe')
- newest: bfloat16 [8192, 512], P('orb', 'probe')
- moments: float32 [4, 512], P(None, 'probe')
Inputs may be any that keep to these rules, and one draw needn't show every extreme that they name: pattern[I, 4] is 1 for every row block; each row block has 4 to 9 ones; the 4 row blocks of one index of orb hold at most 28 ones together, and some index of orb holds exactly 28.
All inputs are finite; a program needn't handle non-finite values.
Results may differ from a plain program's by a relative error of at most 0.0053.
Values may be sent and summed in bfloat16 or wider, within the bound.
A program may use at most 64 MiB of HBM per device.

v0:
```python
import math
import jax
import jax.numpy as jnp
from jax import lax
from jax.sharding import PartitionSpec as P

REACH = 4
STEPS = 4


def extended(array, sides, width):
    for axis, dim in sides:
        peers, length = (lax.axis_size(axis), array.shape[dim])
        up = [(i, (i + 1) % peers) for i in range(peers)]
        down = [(j, i) for i, j in up]
        last = lax.slice_in_dim(array, length - width, length, axis=dim)
        initial = lax.slice_in_dim(array, 0, width, axis=dim)
        before = lax.ppermute(last, axis, up)
        after = lax.ppermute(initial, axis, down)
        array = jnp.concatenate([before, array, after], axis=dim)
    return array


def extend_panel(vec, block_rows):
    return extended(vec, (("orb", 0),), REACH * block_rows)


def body(tiles, pattern, signs, previous, current):
    row_blocks, offsets, shard_rows, block_rows = tiles.shape
    probe_count = previous.shape[1]
    sign_f = (2 * signs - 1).astype(jnp.float32)
    factor = 1.0 / math.sqrt(lax.axis_size("orb") * row_blocks * block_rows)
    full_tiles = lax.all_gather(tiles, "probe", axis=2, tiled=True)
    mask_b = pattern.astype(jnp.bfloat16)
    older, newest = (previous, current)
    collected = []
    for step in range(STEPS):
        blocks = extend_panel(newest, block_rows).reshape(
            row_blocks + 2 * REACH, block_rows, probe_count
        )
        windows = jnp.stack(
            [blocks[offset : offset + row_blocks] for offset in range(offsets)], axis=1
        )
        windows = windows * mask_b[:, :, None, None]
        total = jnp.einsum(
            "roij,rojp->rip", full_tiles, windows, preferred_element_type=jnp.float32
        )
        image = total.reshape(row_blocks * block_rows, probe_count)
        nxt = (2.0 * image - older.astype(jnp.float32)).astype(jnp.bfloat16)
        local_sum = jnp.sum(sign_f * nxt.astype(jnp.float32), axis=0)
        collected.append(lax.psum(local_sum, "orb") * factor)
        older, newest = (newest, nxt)
    stacked = jnp.stack(collected)
    return (older, newest, stacked)


def solution(mesh):
    placed = (
        P("orb", None, "probe", None),
        P("orb", None),
        P("orb", "probe"),
        P("orb", "probe"),
        P("orb", "probe"),
    )
    return jax.shard_map(
        body,
        mesh=mesh,
        in_specs=placed,
        out_specs=(P("orb", "probe"), P("orb", "probe"), P(None, "probe")),
        check_vma=False,
    )
```

profile of v0, /device:TPU:0, one launch (start us, length us, event | category | flops | bytes accessed | tf_op | source)
XLA Modules:
  0.0 224.4 jit_solution(14347151901448904519)
XLA Ops:
  8.4 2.9 %collective-permute-start.1 = (bf16[1024,128]{1,0:T(8,128)(2,1)}, bf16[1024,128]{1,0:T(8,128)(2,1)S(1)}, u32[]{:S(2)}, u32[]{:S(2)}) collective-permute-start(bf16[1024,128]{1,0:T(8,128)(2,1)} %param.9), channel_id=1, source_target_pairs={{4,0},{8,4},{12,8},{16,12},{20,16},{24,20},{28,24},{0,28},{5,1},{9... | collective-permute-start | bytes 786440 | tf_op jit(solution)/shard_map/ppermute | solution.py:19
  11.4 1.1 copy.48
  13.2 2.5 %collective-permute-done = bf16[1024,128]{1,0:T(8,128)(2,1)S(1)} collective-permute-done((bf16[1024,128]{1,0:T(8,128)(2,1)}, bf16[1024,128]{1,0:T(8,128)(2,1)S(1)}, u32[]{:S(2)}, u32[]{:S(2)}) %collective-permute-start) | collective-permute-done | bytes 262176 | tf_op jit(solution)/shard_map/ppermute | solution.py:18
  15.8 1.5 collective-permute-done.1
  23.0 1.1 constant_dynamic-update-slice_fusion.12
  24.1 1.0 constant_dynamic-update-slice_fusion.10
  25.3 76.4 %all-gather.2.cloned.1.call-done = bf16[4,9,256,256]{3,2,1,0:T(8,128)(2,1)} async-done(((bf16[4,9,64,256]{3,2,1,0:T(8,128)(2,1)}), bf16[4,9,256,256]{3,2,1,0:T(8,128)(2,1)}) %all-gather.2.cloned.1.call-update) | async-done | bytes 4718608 | tf_op jit(solution)/shard_map/all_gather | solution.py:33
  101.7 4.0 %fusion.41 = f32[4,256,128]{1,2,0:T(8,128)S(1)} fusion(bf16[4,9,256,256]{3,2,1,0:T(8,128)(2,1)} %all-gather.2.cloned.1.call-done, bf16[4,9,256,128]{2,3,1,0:T(8,128)(2,1)S(1)} %constant_dynamic-update-slice_fusion.4, bf16[4,9]{1,0:T(4,128)(2,1)S(1)} %convert_element_type.38), kind=kOutput, calls=%fused_computation.19 | convolution fusion | flops 605290496 | bytes 7602248 | tf_op jit(solution)/shard_map/roij,rojp->rip/dot_general | solution.py:45
  105.9 1.1 fusion.53
  107.0 2.6 %collective-permute-start.3 = (bf16[1024,128]{1,0:T(8,128)(2,1)S(1)}, bf16[1024,128]{1,0:T(8,128)(2,1)S(1)}, u32[]{:S(2)}, u32[]{:S(2)}) collective-permute-start(bf16[1024,128]{1,0:T(8,128)(2,1)S(1)} %fusion.53), channel_id=1, source_target_pairs={{4,0},{8,4},{12,8},{16,12},{20,16},{24,20},{28,24},{0,28},{5,1},{9... | collective-permute-start | bytes 786440 | tf_op jit(solution)/shard_map/ppermute | solution.py:19
  110.5 4.2 %collective-permute-done.2 = bf16[1024,128]{1,0:T(8,128)(2,1)S(1)} collective-permute-done((bf16[1024,128]{1,0:T(8,128)(2,1)S(1)}, bf16[1024,128]{1,0:T(8,128)(2,1)S(1)}, u32[]{:S(2)}, u32[]{:S(2)}) %collective-permute-start.2) | collective-permute-done | bytes 262176 | tf_op jit(solution)/shard_map/ppermute | solution.py:18
  114.7 1.0 pad_maximum_fusion.4
  118.4 1.8 copy.56
  120.2 1.8 copy.57
  122.0 1.8 copy.59
  123.8 1.8 copy.60
  126.6 1.0 constant_dynamic-update-slice_fusion.20
  127.7 1.0 constant_dynamic-update-slice_fusion.19
  129.6 1.0 constant_dynamic-update-slice_fusion.17
  130.6 1.0 constant_dynamic-update-slice_fusion.16
  131.7 4.0 %fusion.35 = f32[4,256,128]{1,2,0:T(8,128)S(1)} fusion(bf16[4,9,256,256]{3,2,1,0:T(8,128)(2,1)} %all-gather.2.cloned.1.call-done, bf16[4,9,256,128]{2,3,1,0:T(8,128)(2,1)S(1)} %constant_dynamic-update-slice_fusion.13, bf16[4,9]{1,0:T(4,128)(2,1)S(1)} %convert_element_type.38), kind=kOutput, calls=%fused_computation.17 | convolution fusion | flops 605290496 | bytes 7602248 | tf_op jit(solution)/shard_map/roij,rojp->rip/dot_general | solution.py:45
  135.9 1.7 collective-permute-start.4
  137.7 1.1 collective-permute-start.5
  139.6 4.7 %collective-permute-done.4 = bf16[1024,128]{1,0:T(8,128)(2,1)S(1)} collective-permute-done((bf16[1024,128]{1,0:T(8,128)(2,1)S(1)}, bf16[1024,128]{1,0:T(8,128)(2,1)S(1)}, u32[]{:S(2)}, u32[]{:S(2)}) %collective-permute-start.4) | collective-permute-done | bytes 262176 | tf_op jit(solution)/shard_map/ppermute | solution.py:18
  144.4 1.0 pad_maximum_fusion.2
  148.1 1.8 copy.66
  149.9 1.8 copy.67
  151.7 1.8 copy.69
  153.5 1.8 copy.70
  156.3 1.0 constant_dynamic-update-slice_fusion.29
  157.3 1.0 constant_dynamic-update-slice_fusion.28
  159.3 1.0 constant_dynamic-update-slice_fusion.26
  161.3 4.8 %fusion.29 = f32[4,256,128]{1,2,0:T(8,128)} fusion(bf16[4,9,256,256]{3,2,1,0:T(8,128)(2,1)} %all-gather.2.cloned.1.call-done, bf16[4,9,256,128]{2,3,1,0:T(8,128)(2,1)S(1)} %constant_dynamic-update-slice_fusion.22, bf16[4,9]{1,0:T(4,128)(2,1)S(1)} %convert_element_type.38), kind=kOutput, calls=%fused_computation.15 | convolution fusion | flops 605290496 | bytes 7602248 | tf_op jit(solution)/shard_map/roij,rojp->rip/dot_general | solution.py:45
  166.1 1.2 copy.73
  167.5 2.0 collective-permute-start.6
  171.0 5.2 %collective-permute-done.6 = bf16[1024,128]{1,0:T(8,128)(2,1)S(1)} collective-permute-done((bf16[1024,128]{1,0:T(8,128)(2,1)S(1)}, bf16[1024,128]{1,0:T(8,128)(2,1)S(1)}, u32[]{:S(2)}, u32[]{:S(2)}) %collective-permute-start.6) | collective-permute-done | bytes 262176 | tf_op jit(solution)/shard_map/ppermute | solution.py:18
  176.2 1.2 pad_maximum_fusion
  180.0 1.8 copy.76
  181.8 1.8 copy.77
  183.6 1.8 copy.79
  185.4 1.8 copy.80
  187.2 1.8 copy.81
  189.9 1.0 constant_dynamic-update-slice_fusion.38
  190.9 1.0 constant_dynamic-update-slice_fusion.37
  194.9 4.8 %fusion.23 = f32[4,256,128]{1,2,0:T(8,128)} fusion(bf16[4,9,256,256]{3,2,1,0:T(8,128)(2,1)} %all-gather.2.cloned.1.call-done, bf16[4,9,256,128]{2,3,1,0:T(8,128)(2,1)S(1)} %constant_dynamic-update-slice_fusion.31, bf16[4,9]{1,0:T(4,128)(2,1)S(1)} %convert_element_type.38), kind=kOutput, calls=%fused_computation.13 | convolution fusion | flops 605290496 | bytes 7602248 | tf_op jit(solution)/shard_map/roij,rojp->rip/dot_general | solution.py:45
  199.7 1.2 copy.83
  201.0 2.0 fusion.49
  203.0 13.9 %all-reduce = (f32[128]{0:T(128)S(1)}, f32[128]{0:T(128)S(1)}, f32[128]{0:T(128)S(1)}, f32[128]{0:T(128)S(1)}) all-reduce(f32[128]{0:T(128)S(1)} %get-tuple-element.4, f32[128]{0:T(128)S(1)} %get-tuple-element.5, f32[128]{0:T(128)S(1)} %get-tuple-element.6, f32[128]{0:T(128)S(1)} %get-tuple-element.3), channel_id=1, replica_groups=mesh['orb'=8,'probe'=4] {'orb'}, use_global_device_ids=true, to_apply=%region_7.0 | all-reduce | flops 512 | bytes 4096 | tf_op jit(solution)/shard_map/psum | solution.py:51
  (95 shorter events, 29.1 us)
Async XLA Ops:
  7.2 8.6 %copy-start.1 = (bf16[1024,128]{1,0:T(8,128)(2,1)S(1)}, bf16[1024,128]{1,0:T(8,128)(2,1)}, u32[]{:S(2)}) copy-start(bf16[1024,128]{1,0:T(8,128)(2,1)} %param.9) | copy-start | bytes 786436
  7.2 94.5 %all-gather.2.cloned.1.call-start = ((), (), s32[]{:S(2)}) async-start(), calls=%async_computation | async-start | bytes 5898240 | tf_op jit(solution)/shard_map/all_gather | solution.py:33
  7.9 7.8 %collective-permute-start = (bf16[1024,128]{1,0:T(8,128)(2,1)}, bf16[1024,128]{1,0:T(8,128)(2,1)S(1)}, u32[]{:S(2)}, u32[]{:S(2)}) collective-permute-start(bf16[1024,128]{1,0:T(8,128)(2,1)} %param.9), channel_id=1, source_target_pairs={{0,4},{4,8},{8,12},{12,16},{16,20},{20,24},{24,28},{28,0},{1,5},{5... | collective-permute-start | bytes 786440 | tf_op jit(solution)/shard_map/ppermute | solution.py:18
  8.4 8.9 %collective-permute-start.1 = (bf16[1024,128]{1,0:T(8,128)(2,1)}, bf16[1024,128]{1,0:T(8,128)(2,1)S(1)}, u32[]{:S(2)}, u32[]{:S(2)}) collective-permute-start(bf16[1024,128]{1,0:T(8,128)(2,1)} %param.9), channel_id=1, source_target_pairs={{4,0},{8,4},{12,8},{16,12},{20,16},{24,20},{28,24},{0,28},{5,1},{9... | collective-permute-start | bytes 786440 | tf_op jit(solution)/shard_map/ppermute | solution.py:19
  23.0 2.1 copy-start.5
  23.0 2.2 copy-start.3
  23.0 2.2 copy-start.4
  23.0 2.2 copy-start.2
  107.0 7.7 %collective-permute-start.2 = (bf16[1024,128]{1,0:T(8,128)(2,1)S(1)}, bf16[1024,128]{1,0:T(8,128)(2,1)S(1)}, u32[]{:S(2)}, u32[]{:S(2)}) collective-permute-start(bf16[1024,128]{1,0:T(8,128)(2,1)S(1)} %fusion.53), channel_id=1, source_target_pairs={{0,4},{4,8},{8,12},{12,16},{16,20},{20,24},{24,28},{28,0},{1,5},{5... | collective-permute-start | bytes 786440 | tf_op jit(solution)/shard_map/ppermute | solution.py:18
  107.0 7.7 %collective-permute-start.3 = (bf16[1024,128]{1,0:T(8,128)(2,1)S(1)}, bf16[1024,128]{1,0:T(8,128)(2,1)S(1)}, u32[]{:S(2)}, u32[]{:S(2)}) collective-permute-start(bf16[1024,128]{1,0:T(8,128)(2,1)S(1)} %fusion.53), channel_id=1, source_target_pairs={{4,0},{8,4},{12,8},{16,12},{20,16},{24,20},{28,24},{0,28},{5,1},{9... | collective-permute-start | bytes 786440 | tf_op jit(solution)/shard_map/ppermute | solution.py:19
  126.6 4.9 %copy-start.7 = (bf16[4,1,256,128]{2,3,1,0:T(8,128)(2,1)S(1)}, bf16[4,1,256,128]{2,3,1,0:T(8,128)(2,1)}, u32[]{:S(2)}) copy-start(bf16[4,1,256,128]{2,3,1,0:T(8,128)(2,1)} %copy.60) | copy-start | bytes 786436
  126.6 5.0 %copy-start.8 = (bf16[4,1,256,128]{2,3,1,0:T(8,128)(2,1)S(1)}, bf16[4,1,256,128]{2,3,1,0:T(8,128)(2,1)}, u32[]{:S(2)}) copy-start(bf16[4,1,256,128]{2,3,1,0:T(8,128)(2,1)} %copy.61) | copy-start | bytes 786436
  135.9 8.4 %collective-permute-start.4 = (bf16[1024,128]{1,0:T(8,128)(2,1)S(1)}, bf16[1024,128]{1,0:T(8,128)(2,1)S(1)}, u32[]{:S(2)}, u32[]{:S(2)}) collective-permute-start(bf16[1024,128]{1,0:T(8,128)(2,1)S(1)} %fusion.52), channel_id=1, source_target_pairs={{0,4},{4,8},{8,12},{12,16},{16,20},{20,24},{24,28},{28,0},{1,5},{5... | collective-permute-start | bytes 786440 | tf_op jit(solution)/shard_map/ppermute | solution.py:18
  137.7 6.7 %collective-permute-start.5 = (bf16[1024,128]{1,0:T(8,128)(2,1)S(1)}, bf16[1024,128]{1,0:T(8,128)(2,1)S(1)}, u32[]{:S(2)}, u32[]{:S(2)}) collective-permute-start(bf16[1024,128]{1,0:T(8,128)(2,1)S(1)} %fusion.52), channel_id=1, source_target_pairs={{4,0},{8,4},{12,8},{16,12},{20,16},{24,20},{28,24},{0,28},{5,1},{9... | collective-permute-start | bytes 786440 | tf_op jit(solution)/shard_map/ppermute | solution.py:19
  156.3 4.9 %copy-start.9 = (bf16[4,1,256,128]{2,3,1,0:T(8,128)(2,1)S(1)}, bf16[4,1,256,128]{2,3,1,0:T(8,128)(2,1)}, u32[]{:S(2)}) copy-start(bf16[4,1,256,128]{2,3,1,0:T(8,128)(2,1)} %copy.70) | copy-start | bytes 786436
  156.3 5.0 %copy-start.10 = (bf16[4,1,256,128]{2,3,1,0:T(8,128)(2,1)S(1)}, bf16[4,1,256,128]{2,3,1,0:T(8,128)(2,1)}, u32[]{:S(2)}) copy-start(bf16[4,1,256,128]{2,3,1,0:T(8,128)(2,1)} %copy.71) | copy-start | bytes 786436
  167.4 33.5 %copy-start = (bf16[1024,128]{1,0:T(8,128)(2,1)}, bf16[1024,128]{1,0:T(8,128)(2,1)S(1)}, u32[]{:S(2)}) copy-start(bf16[1024,128]{1,0:T(8,128)(2,1)S(1)} %fusion.48) | copy-start | bytes 786436
  167.5 8.7 %collective-permute-start.6 = (bf16[1024,128]{1,0:T(8,128)(2,1)S(1)}, bf16[1024,128]{1,0:T(8,128)(2,1)S(1)}, u32[]{:S(2)}, u32[]{:S(2)}) collective-permute-start(bf16[1024,128]{1,0:T(8,128)(2,1)S(1)} %fusion.48), channel_id=1, source_target_pairs={{0,4},{4,8},{8,12},{12,16},{16,20},{20,24},{24,28},{28,0},{1,5},{5... | collective-permute-start | bytes 786440 | tf_op jit(solution)/shard_map/ppermute | solution.py:18
  169.5 6.7 %collective-permute-start.7 = (bf16[1024,128]{1,0:T(8,128)(2,1)S(1)}, bf16[1024,128]{1,0:T(8,128)(2,1)S(1)}, u32[]{:S(2)}, u32[]{:S(2)}) collective-permute-start(bf16[1024,128]{1,0:T(8,128)(2,1)S(1)} %fusion.48), channel_id=1, source_target_pairs={{4,0},{8,4},{12,8},{16,12},{20,16},{24,20},{28,24},{0,28},{5,1},{9... | collective-permute-start | bytes 786440 | tf_op jit(solution)/shard_map/ppermute | solution.py:19
  189.9 4.9 %copy-start.11 = (bf16[4,1,256,128]{2,3,1,0:T(8,128)(2,1)S(1)}, bf16[4,1,256,128]{2,3,1,0:T(8,128)(2,1)}, u32[]{:S(2)}) copy-start(bf16[4,1,256,128]{2,3,1,0:T(8,128)(2,1)} %copy.80) | copy-start | bytes 786436
  189.9 5.0 %copy-start.12 = (bf16[4,1,256,128]{2,3,1,0:T(8,128)(2,1)S(1)}, bf16[4,1,256,128]{2,3,1,0:T(8,128)(2,1)}, u32[]{:S(2)}) copy-start(bf16[4,1,256,128]{2,3,1,0:T(8,128)(2,1)} %copy.81) | copy-start | bytes 786436
  189.9 5.0 %copy-start.6 = (bf16[4,1,256,128]{2,3,1,0:T(8,128)(2,1)S(1)}, bf16[4,1,256,128]{2,3,1,0:T(8,128)(2,1)}, u32[]{:S(2)}) copy-start(bf16[4,1,256,128]{2,3,1,0:T(8,128)(2,1)} %copy.82) | copy-start | bytes 786436
Sparse Core Ops, SparseCore 0:
  9.6 92.0 all-gather.1
where the time goes:
time: 226 us; the launch traced here: 224 us
  waiting for transfers between devices  95.2 us (42%)
  local copies, waits for them, and re-layouts  63.6 us (28%)
  matrix products  17.6 us (8%)
  between operations  14.6 us (6%)
  blocking collectives  13.9 us (6%)
  starting transfers between devices  11.7 us (5%)
  other arithmetic  7.73 us (3%)
    all_gather x1, waiting for transfers between devices, body(): full_tiles = lax.all_gather(tiles, 'probe', axis=2, tiled=True)  76.4 us
    another operation x40, local copies, waits for them, and re-layouts, body(): jnp.stack([blocks[offset:offset + row_blocks] for offset in range(offsets...  40.6 us
    unnamed x60, local copies, waits for them, and re-layouts  20 us
    dot_general x4, matrix products, body(): jnp.einsum('roij,rojp->rip', full_tiles, windows, preferred_element_type=...  17.6 us
    ppermute x4, waiting for transfers between devices, extended(): before = lax.ppermute(last, axis, up)  16.6 us
    psum x1, blocking collectives, body(): collected.append(lax.psum(local_sum, 'orb') * factor)  13.9 us
    ppermute x4, starting transfers between devices, extended(): after = lax.ppermute(initial, axis, down)  7.37 us
  transfers between devices with their start and end apart: 9, of which 6 were waited for; matrix products, arithmetic and copies ran while one was open for 5% of the time, Pallas kernels for 0%

commit v1 on v0

--- a/solution.py
+++ b/solution.py
@@ -1,11 +1,36 @@
+import functools
 import math
 import jax
 import jax.numpy as jnp
 from jax import lax
 from jax.sharding import PartitionSpec as P
+from jax.lax import axis_index, axis_size, ppermute
 
 REACH = 4
 STEPS = 4
+
+
+def list_skins(shard_in, along_axis, row_dim):
+    parts_seen = [shard_in]
+    amount_of = axis_size(along_axis)
+    h = 0
+    while h < amount_of - 1:
+        parts_seen.append(
+            ppermute(
+                parts_seen[-1],
+                along_axis,
+                perm=[(j0, (j0 + 1) % amount_of) for j0 in range(amount_of)],
+            )
+        )
+        h = h + 1
+    return jnp.roll(
+        jnp.concatenate(parts_seen[::-1], row_dim),
+        (axis_index(along_axis) + 1) * shard_in.shape[row_dim],
+        row_dim,
+    )
+
+
+_follow_chunk = functools.partial(list_skins, along_axis="probe", row_dim=2)
 
 
 def extended(array, sides, width):
@@ -30,7 +55,7 @@
     probe_count = previous.shape[1]
     sign_f = (2 * signs - 1).astype(jnp.float32)
     factor = 1.0 / math.sqrt(lax.axis_size("orb") * row_blocks * block_rows)
-    full_tiles = lax.all_gather(tiles, "probe", axis=2, tiled=True)
+    full_tiles = _follow_chunk(tiles)
     mask_b = pattern.astype(jnp.bfloat16)
     older, newest = (previous, current)
     collected = []

time: 226 us -> 139 us (0.62)
  local copies, waits for them, and re-layouts: 63.6 us -> 4.42 us
  between operations: 14.6 us -> 1.16 us
  matrix products: 17.6 us -> 5.82 us
  other arithmetic: 7.73 us -> 3.02 us
  waiting for transfers between devices: 95.2 us -> 98.7 us
    all_gather x1 -> x0, waiting for transfers between devices: 76.4 us -> none  [body(): full_tiles = lax.all_gather(tiles, 'probe', axis=2, tiled=True)]
    ppermute x0 -> x3, waiting for transfers between devices: none -> 75.6 us  [list_skins(): ppermute(parts_seen[-1], along_axis, perm=[(j0, (j0 + 1) % amount_of) for...]
    another operation x40 -> x4, local copies, waits for them, and re-layouts: 40.6 us -> 0.15 us  [body(): jnp.stack([blocks[offset:offset + row_blocks] for offset in range(offsets...]
    unnamed x60 -> x51, local copies, waits for them, and re-layouts: 20 us -> 3.97 us
    dot_general x4, matrix products: 17.6 us -> 5.82 us  [body(): jnp.einsum('roij,rojp->rip', full_tiles, windows, preferred_element_type=...]
    ppermute x4, waiting for transfers between devices: 16.6 us -> 23.1 us  [extended(): before = lax.ppermute(last, axis, up)]
    ppermute x0 -> x3, starting transfers between devices: none -> 3.08 us  [list_skins(): ppermute(parts_seen[-1], along_axis, perm=[(j0, (j0 + 1) % amount_of) for...]
    ppermute x4, starting transfers between devices: 4.31 us -> 1.27 us  [extended(): before = lax.ppermute(last, axis, up)]
  transfers between devices with their start and end apart: 9 -> 11, of which waited for: 6 -> 7; matrix products, arithmetic and copies ran while one was open for 5% -> 2% of each run, Pallas kernels for 0% -> 0%
where the time goes in v1:
time: 139 us
  waiting for transfers between devices  98.7 us (71%)
  starting transfers between devices  13.8 us (10%)
  blocking collectives  11.8 us (8%)
  matrix products  5.82 us (4%)
  local copies, waits for them, and re-layouts  4.42 us (3%)
  other arithmetic  3.02 us (2%)
    ppermute x3, waiting for transfers between devices, list_skins(): ppermute(parts_seen[-1], along_axis, perm=[(j0, (j0 + 1) % amount_of) for...  75.6 us
    ppermute x4, waiting for transfers between devices, extended(): before = lax.ppermute(last, axis, up)  23.1 us
    psum x1, blocking collectives, body(): collected.append(lax.psum(local_sum, 'orb') * factor)  11.8 us
    ppermute x4, starting transfers between devices, extended(): after = lax.ppermute(initial, axis, down)  9.46 us
    dot_general x4, matrix products, body(): jnp.einsum('roij,rojp->rip', full_tiles, windows, preferred_element_type=...  5.82 us
    unnamed x51, local copies, waits for them, and re-layouts  3.97 us
    ppermute x3, starting transfers between devices, list_skins(): ppermute(parts_seen[-1], along_axis, perm=[(j0, (j0 + 1) % amount_of) for...  3.08 us
  transfers between devices with their start and end apart: 11, of which 7 were waited for; matrix products, arithmetic and copies ran while one was open for 2% of the time, Pallas kernels for 0%

profile of v1, /device:TPU:0, one launch (start us, length us, event | category | flops | bytes accessed | tf_op | source)
XLA Modules:
  0.0 138.7 jit_solution(6313543482221781230)
XLA Ops:
  0.6 3.1 %collective-permute-start = (bf16[4,9,64,256]{3,2,1,0:T(8,128)(2,1)}, bf16[4,9,64,256]{3,2,1,0:T(8,128)(2,1)S(1)}, u32[]{:S(2)}, u32[]{:S(2)}) collective-permute-start(bf16[4,9,64,256]{3,2,1,0:T(8,128)(2,1)} %param.5), channel_id=1, source_target_pairs={{0,1},{1,2},{2,3},{3,0},{4,5},{5,6},{6,7},{7,4},{8,9},{9,10},{10,1... | collective-permute-start | bytes 3538952 | tf_op jit(solution)/shard_map/ppermute | solution.py:19
  3.7 28.2 %collective-permute-done = bf16[4,9,64,256]{3,2,1,0:T(8,128)(2,1)S(1)} collective-permute-done((bf16[4,9,64,256]{3,2,1,0:T(8,128)(2,1)}, bf16[4,9,64,256]{3,2,1,0:T(8,128)(2,1)S(1)}, u32[]{:S(2)}, u32[]{:S(2)}) %collective-permute-start) | collective-permute-done | bytes 1179680 | tf_op jit(solution)/shard_map/ppermute | solution.py:19
  31.9 0.0 collective-permute-start.1
  31.9 0.0 collective-permute-start.3
  31.9 2.6 %collective-permute-start.4 = (bf16[1024,128]{1,0:T(8,128)(2,1)}, bf16[1024,128]{1,0:T(8,128)(2,1)S(1)}, u32[]{:S(2)}, u32[]{:S(2)}) collective-permute-start(bf16[1024,128]{1,0:T(8,128)(2,1)} %param.9), channel_id=1, source_target_pairs={{4,0},{8,4},{12,8},{16,12},{20,16},{24,20},{28,24},{0,28},{5,1},{9... | collective-permute-start | bytes 786440 | tf_op jit(solution)/shard_map/ppermute | solution.py:44
  34.6 0.7 convert_element_type.38
  35.2 4.5 %collective-permute-done.3 = bf16[1024,128]{1,0:T(8,128)(2,1)S(1)} collective-permute-done((bf16[1024,128]{1,0:T(8,128)(2,1)}, bf16[1024,128]{1,0:T(8,128)(2,1)S(1)}, u32[]{:S(2)}, u32[]{:S(2)}) %collective-permute-start.3) | collective-permute-done | bytes 262176 | tf_op jit(solution)/shard_map/ppermute | solution.py:43
  39.8 0.0 copy-start.2
  39.8 1.1 constant_dynamic-update-slice_fusion.11
  40.9 0.1 fusion.80
  41.0 19.8 %collective-permute-done.1 = bf16[4,9,64,256]{3,2,1,0:T(8,128)(2,1)S(1)} collective-permute-done((bf16[4,9,64,256]{3,2,1,0:T(8,128)(2,1)S(1)}, bf16[4,9,64,256]{3,2,1,0:T(8,128)(2,1)S(1)}, u32[]{:S(2)}, u32[]{:S(2)}) %collective-permute-start.1) | collective-permute-done | bytes 1179680 | tf_op jit(solution)/shard_map/ppermute | solution.py:19
  61.0 0.1 fusion.79
  61.3 27.6 %collective-permute-done.2 = bf16[4,9,64,256]{3,2,1,0:T(8,128)(2,1)S(1)} collective-permute-done((bf16[4,9,64,256]{3,2,1,0:T(8,128)(2,1)S(1)}, bf16[4,9,64,256]{3,2,1,0:T(8,128)(2,1)S(1)}, u32[]{:S(2)}, u32[]{:S(2)}) %collective-permute-start.2) | collective-permute-done | bytes 1179680 | tf_op jit(solution)/shard_map/ppermute | solution.py:19
  88.9 0.1 constant_dynamic-update-slice_fusion.7
  89.0 0.0 copy-start
  89.0 0.1 constant_dynamic-update-slice_fusion.6
  89.1 0.1 constant_dynamic-update-slice_fusion.5
  89.2 1.0 copy-done
  90.3 0.1 constant_dynamic-update-slice_fusion.4
  90.3 0.1 constant_dynamic-update-slice_fusion.3
  90.4 0.1 constant_dynamic-update-slice_fusion.2
  90.5 0.1 constant_dynamic-update-slice_fusion.1
  90.7 0.1 constant_dynamic-update-slice_fusion
  90.8 0.0 copy-start.4
  90.8 1.5 %fusion.47 = f32[4,256,128]{2,1,0:T(8,128)S(1)} fusion(bf16[4,9,256,128]{3,2,1,0:T(8,128)(2,1)S(1)} %constant_dynamic-update-slice_fusion.12, bf16[4,9,512,256]{3,2,1,0:T(8,128)(2,1)S(1)} %constant_dynamic-update-slice_fusion, s32[]{:T(128)S(6)} %select_n.14, bf16[4,9]{1,0:T(4,128)(2,1)S(1)} %convert_element_type.38), kind=kOutput, calls=%fused_computation.19 | convolution fusion | flops 605290496 | bytes 7603204 | tf_op jit(solution)/shard_map/roij,rojp->rip/dot_general | solution.py:70
  92.2 0.1 fusion.61
  92.3 0.1 collective-permute-start.5
  92.4 2.6 %collective-permute-start.6 = (bf16[1024,128]{1,0:T(8,128)(2,1)S(1)}, bf16[1024,128]{1,0:T(8,128)(2,1)S(1)}, u32[]{:S(2)}, u32[]{:S(2)}) collective-permute-start(bf16[1024,128]{1,0:T(8,128)(2,1)S(1)} %fusion.61), channel_id=1, source_target_pairs={{4,0},{8,4},{12,8},{16,12},{20,16},{24,20},{28,24},{0,28},{5,1},{9... | collective-permute-start | bytes 786440 | tf_op jit(solution)/shard_map/ppermute | solution.py:44
  95.0 5.4 %collective-permute-done.5 = bf16[1024,128]{1,0:T(8,128)(2,1)S(1)} collective-permute-done((bf16[1024,128]{1,0:T(8,128)(2,1)S(1)}, bf16[1024,128]{1,0:T(8,128)(2,1)S(1)}, u32[]{:S(2)}, u32[]{:S(2)}) %collective-permute-start.5) | collective-permute-done | bytes 262176 | tf_op jit(solution)/shard_map/ppermute | solution.py:43
  100.5 0.2 pad_maximum_fusion.4
  101.0 1.5 %fusion.42 = f32[4,256,128]{2,1,0:T(8,128)S(1)} fusion(bf16[4,9,256,128]{3,2,1,0:T(8,128)(2,1)S(1)} %constant_dynamic-update-slice_fusion.21, bf16[4,9,512,256]{3,2,1,0:T(8,128)(2,1)S(1)} %constant_dynamic-update-slice_fusion, s32[]{:T(128)S(6)} %select_n.14, bf16[4,9]{1,0:T(4,128)(2,1)S(1)} %convert_element_type.38), kind=kOutput, calls=%fused_computation.18 | convolution fusion | flops 605290496 | bytes 7603204 | tf_op jit(solution)/shard_map/roij,rojp->rip/dot_general | solution.py:70
  102.5 0.1 fusion.60
  102.6 0.8 collective-permute-start.7
  103.4 1.9 %collective-permute-start.8 = (bf16[1024,128]{1,0:T(8,128)(2,1)S(1)}, bf16[1024,128]{1,0:T(8,128)(2,1)S(1)}, u32[]{:S(2)}, u32[]{:S(2)}) collective-permute-start(bf16[1024,128]{1,0:T(8,128)(2,1)S(1)} %fusion.60), channel_id=1, source_target_pairs={{4,0},{8,4},{12,8},{16,12},{20,16},{24,20},{28,24},{0,28},{5,1},{9... | collective-permute-start | bytes 786440 | tf_op jit(solution)/shard_map/ppermute | solution.py:44
  105.3 6.4 %collective-permute-done.7 = bf16[1024,128]{1,0:T(8,128)(2,1)S(1)} collective-permute-done((bf16[1024,128]{1,0:T(8,128)(2,1)S(1)}, bf16[1024,128]{1,0:T(8,128)(2,1)S(1)}, u32[]{:S(2)}, u32[]{:S(2)}) %collective-permute-start.7) | collective-permute-done | bytes 262176 | tf_op jit(solution)/shard_map/ppermute | solution.py:43
  111.7 0.2 pad_maximum_fusion.2
  112.2 1.5 %fusion.37 = f32[4,256,128]{2,1,0:T(8,128)S(1)} fusion(bf16[4,9,256,128]{3,2,1,0:T(8,128)(2,1)S(1)} %constant_dynamic-update-slice_fusion.30, bf16[4,9,512,256]{3,2,1,0:T(8,128)(2,1)S(1)} %constant_dynamic-update-slice_fusion, s32[]{:T(128)S(6)} %select_n.14, bf16[4,9]{1,0:T(4,128)(2,1)S(1)} %convert_element_type.38), kind=kOutput, calls=%fused_computation.17 | convolution fusion | flops 605290496 | bytes 7603204 | tf_op jit(solution)/shard_map/roij,rojp->rip/dot_general | solution.py:70
  113.7 0.1 fusion.56
  113.7 0.0 copy-start.1
  113.8 0.4 collective-permute-start.9
  114.1 2.3 %collective-permute-start.10 = (bf16[1024,128]{1,0:T(8,128)(2,1)S(1)}, bf16[1024,128]{1,0:T(8,128)(2,1)S(1)}, u32[]{:S(2)}, u32[]{:S(2)}) collective-permute-start(bf16[1024,128]{1,0:T(8,128)(2,1)S(1)} %fusion.56), channel_id=1, source_target_pairs={{4,0},{8,4},{12,8},{16,12},{20,16},{24,20},{28,24},{0,28},{5,1},{9... | collective-permute-start | bytes 786440 | tf_op jit(solution)/shard_map/ppermute | solution.py:44
  116.4 6.8 %collective-permute-done.9 = bf16[1024,128]{1,0:T(8,128)(2,1)S(1)} collective-permute-done((bf16[1024,128]{1,0:T(8,128)(2,1)S(1)}, bf16[1024,128]{1,0:T(8,128)(2,1)S(1)}, u32[]{:S(2)}, u32[]{:S(2)}) %collective-permute-start.9) | collective-permute-done | bytes 262176 | tf_op jit(solution)/shard_map/ppermute | solution.py:43
  123.2 0.2 pad_maximum_fusion
  123.8 0.0 copy-start.3
  123.8 1.5 %fusion.32 = f32[4,256,128]{2,1,0:T(8,128)S(1)} fusion(bf16[4,9,256,128]{3,2,1,0:T(8,128)(2,1)S(1)} %constant_dynamic-update-slice_fusion.39, bf16[4,9,512,256]{3,2,1,0:T(8,128)(2,1)S(1)} %constant_dynamic-update-slice_fusion, s32[]{:T(128)S(6)} %select_n.14, bf16[4,9]{1,0:T(4,128)(2,1)S(1)} %convert_element_type.38), kind=kOutput, calls=%fused_computation.16 | convolution fusion | flops 605290496 | bytes 7603204 | tf_op jit(solution)/shard_map/roij,rojp->rip/dot_general | solution.py:70
  125.3 1.0 fusion.57
  126.3 11.8 %all-reduce = (f32[128]{0:T(128)S(1)}, f32[128]{0:T(128)S(1)}, f32[128]{0:T(128)S(1)}, f32[128]{0:T(128)S(1)}) all-reduce(f32[128]{0:T(128)S(1)} %get-tuple-element.4, f32[128]{0:T(128)S(1)} %get-tuple-element.5, f32[128]{0:T(128)S(1)} %get-tuple-element.6, f32[128]{0:T(128)S(1)} %get-tuple-element.3), channel_id=1, replica_groups=mesh['orb'=8,'probe'=4] {'orb'}, use_global_device_ids=true, to_apply=%region_7.8 | all-reduce | flops 512 | bytes 4096 | tf_op jit(solution)/shard_map/psum | solution.py:76
  138.1 0.6 pad_maximum_fusion.6
  (50 shorter events, 1.3 us)
Async XLA Ops:
  0.6 31.3 %collective-permute-start = (bf16[4,9,64,256]{3,2,1,0:T(8,128)(2,1)}, bf16[4,9,64,256]{3,2,1,0:T(8,128)(2,1)S(1)}, u32[]{:S(2)}, u32[]{:S(2)}) collective-permute-start(bf16[4,9,64,256]{3,2,1,0:T(8,128)(2,1)} %param.5), channel_id=1, source_target_pairs={{0,1},{1,2},{2,3},{3,0},{4,5},{5,6},{6,7},{7,4},{8,9},{9,10},{10,1... | collective-permute-start | bytes 3538952 | tf_op jit(solution)/shard_map/ppermute | solution.py:19
  31.9 29.0 %collective-permute-start.1 = (bf16[4,9,64,256]{3,2,1,0:T(8,128)(2,1)S(1)}, bf16[4,9,64,256]{3,2,1,0:T(8,128)(2,1)S(1)}, u32[]{:S(2)}, u32[]{:S(2)}) collective-permute-start(bf16[4,9,64,256]{3,2,1,0:T(8,128)(2,1)S(1)} %collective-permute-done), channel_id=1, source_target_pairs={{0,1},{1,2},{2,3},{3,0},{4,5},{5,6},{6,7},{7,4},{8,9},{9,10},{10,1... | collective-permute-start | bytes 3538952 | tf_op jit(solution)/shard_map/ppermute | solution.py:19
  31.9 7.8 %collective-permute-start.3 = (bf16[1024,128]{1,0:T(8,128)(2,1)}, bf16[1024,128]{1,0:T(8,128)(2,1)S(1)}, u32[]{:S(2)}, u32[]{:S(2)}) collective-permute-start(bf16[1024,128]{1,0:T(8,128)(2,1)} %param.9), channel_id=1, source_target_pairs={{0,4},{4,8},{8,12},{12,16},{16,20},{20,24},{24,28},{28,0},{1,5},{5... | collective-permute-start | bytes 786440 | tf_op jit(solution)/shard_map/ppermute | solution.py:43
  31.9 9.0 %collective-permute-start.4 = (bf16[1024,128]{1,0:T(8,128)(2,1)}, bf16[1024,128]{1,0:T(8,128)(2,1)S(1)}, u32[]{:S(2)}, u32[]{:S(2)}) collective-permute-start(bf16[1024,128]{1,0:T(8,128)(2,1)} %param.9), channel_id=1, source_target_pairs={{4,0},{8,4},{12,8},{16,12},{20,16},{24,20},{28,24},{0,28},{5,1},{9... | collective-permute-start | bytes 786440 | tf_op jit(solution)/shard_map/ppermute | solution.py:44
  39.8 21.2 %copy-start.2 = (bf16[1024,128]{1,0:T(8,128)(2,1)S(1)}, bf16[1024,128]{1,0:T(8,128)(2,1)}, u32[]{:S(2)}) copy-start(bf16[1024,128]{1,0:T(8,128)(2,1)} %param.9) | copy-start | bytes 786436
  60.9 28.0 %collective-permute-start.2 = (bf16[4,9,64,256]{3,2,1,0:T(8,128)(2,1)S(1)}, bf16[4,9,64,256]{3,2,1,0:T(8,128)(2,1)S(1)}, u32[]{:S(2)}, u32[]{:S(2)}) collective-permute-start(bf16[4,9,64,256]{3,2,1,0:T(8,128)(2,1)S(1)} %collective-permute-done.1), channel_id=1, source_target_pairs={{0,1},{1,2},{2,3},{3,0},{4,5},{5,6},{6,7},{7,4},{8,9},{9,10},{10,1... | collective-permute-start | bytes 3538952 | tf_op jit(solution)/shard_map/ppermute | solution.py:19
  89.0 1.3 copy-start
  90.8 1.5 %copy-start.4 = (bf16[1024,128]{1,0:T(8,128)(2,1)S(1)}, bf16[1024,128]{1,0:T(8,128)(2,1)}, u32[]{:S(2)}) copy-start(bf16[1024,128]{1,0:T(8,128)(2,1)} %param.8) | copy-start | bytes 786436
  92.3 8.1 %collective-permute-start.5 = (bf16[1024,128]{1,0:T(8,128)(2,1)S(1)}, bf16[1024,128]{1,0:T(8,128)(2,1)S(1)}, u32[]{:S(2)}, u32[]{:S(2)}) collective-permute-start(bf16[1024,128]{1,0:T(8,128)(2,1)S(1)} %fusion.61), channel_id=1, source_target_pairs={{0,4},{4,8},{8,12},{12,16},{16,20},{20,24},{24,28},{28,0},{1,5},{5... | collective-permute-start | bytes 786440 | tf_op jit(solution)/shard_map/ppermute | solution.py:43
  92.4 8.1 %collective-permute-start.6 = (bf16[1024,128]{1,0:T(8,128)(2,1)S(1)}, bf16[1024,128]{1,0:T(8,128)(2,1)S(1)}, u32[]{:S(2)}, u32[]{:S(2)}) collective-permute-start(bf16[1024,128]{1,0:T(8,128)(2,1)S(1)} %fusion.61), channel_id=1, source_target_pairs={{4,0},{8,4},{12,8},{16,12},{20,16},{24,20},{28,24},{0,28},{5,1},{9... | collective-permute-start | bytes 786440 | tf_op jit(solution)/shard_map/ppermute | solution.py:44
  102.6 9.1 %collective-permute-start.7 = (bf16[1024,128]{1,0:T(8,128)(2,1)S(1)}, bf16[1024,128]{1,0:T(8,128)(2,1)S(1)}, u32[]{:S(2)}, u32[]{:S(2)}) collective-permute-start(bf16[1024,128]{1,0:T(8,128)(2,1)S(1)} %fusion.60), channel_id=1, source_target_pairs={{0,4},{4,8},{8,12},{12,16},{16,20},{20,24},{24,28},{28,0},{1,5},{5... | collective-permute-start | bytes 786440 | tf_op jit(solution)/shard_map/ppermute | solution.py:43
  103.4 8.3 %collective-permute-start.8 = (bf16[1024,128]{1,0:T(8,128)(2,1)S(1)}, bf16[1024,128]{1,0:T(8,128)(2,1)S(1)}, u32[]{:S(2)}, u32[]{:S(2)}) collective-permute-start(bf16[1024,128]{1,0:T(8,128)(2,1)S(1)} %fusion.60), channel_id=1, source_target_pairs={{4,0},{8,4},{12,8},{16,12},{20,16},{24,20},{28,24},{0,28},{5,1},{9... | collective-permute-start | bytes 786440 | tf_op jit(solution)/shard_map/ppermute | solution.py:44
  113.7 11.6 %copy-start.1 = (bf16[1024,128]{1,0:T(8,128)(2,1)}, bf16[1024,128]{1,0:T(8,128)(2,1)S(1)}, u32[]{:S(2)}) copy-start(bf16[1024,128]{1,0:T(8,128)(2,1)S(1)} %fusion.56) | copy-start | bytes 786436
  113.8 9.5 %collective-permute-start.9 = (bf16[1024,128]{1,0:T(8,128)(2,1)S(1)}, bf16[1024,128]{1,0:T(8,128)(2,1)S(1)}, u32[]{:S(2)}, u32[]{:S(2)}) collective-permute-start(bf16[1024,128]{1,0:T(8,128)(2,1)S(1)} %fusion.56), channel_id=1, source_target_pairs={{0,4},{4,8},{8,12},{12,16},{16,20},{20,24},{24,28},{28,0},{1,5},{5... | collective-permute-start | bytes 786440 | tf_op jit(solution)/shard_map/ppermute | solution.py:43
  114.1 9.1 %collective-permute-start.10 = (bf16[1024,128]{1,0:T(8,128)(2,1)S(1)}, bf16[1024,128]{1,0:T(8,128)(2,1)S(1)}, u32[]{:S(2)}, u32[]{:S(2)}) collective-permute-start(bf16[1024,128]{1,0:T(8,128)(2,1)S(1)} %fusion.56), channel_id=1, source_target_pairs={{4,0},{8,4},{12,8},{16,12},{20,16},{24,20},{28,24},{0,28},{5,1},{9... | collective-permute-start | bytes 786440 | tf_op jit(solution)/shard_map/ppermute | solution.py:44
  123.8 1.5 %copy-start.3 = (s32[1024,128]{1,0:T(8,128)S(1)}, s32[1024,128]{1,0:T(8,128)}, u32[]{:S(2)}) copy-start(s32[1024,128]{1,0:T(8,128)} %param.7) | copy-start | bytes 1572868
